TPU v7x, 256 devices: a whole 4x4x8 slice. The times are simulated.
256 devices in a mesh: row: 8 (over x_lo, y), col: 16 (over z, core), layer: 2 (over x_hi).
Axes of the slice: x: 4 (x_hi: 2, x_lo: 2; x = x_hi * 2 + x_lo), y: 4, z: 8, core: 2. Of those that a mesh axis runs over, the one named last changes fastest.
Arguments:
- density: float32 [4096, 4096], P('row', ('col', 'layer')), may hold values from -1 to 1, as said below
- pattern: int32 [32, 32], replicated, may hold values from 0 to 1, as said below
Outputs:
- purified: float32 [4096, 4096], P('row', ('col', 'layer'))
Inputs may be any that keep to these rules, and one draw needn't show every extreme that they name: pattern is symmetric, with ones on its diagonal; its entries are 0 or 1. density is symmetric.
All inputs are finite; a program needn't handle non-finite values.
Results may differ from a plain program's by a relative error of at most 0.00018.
Values sent between devices are 32-bit elements; how exact they have to be, the bound alone decides.
No kernel may reach another device: no remote copies, remote signals or barrier semaphores. Data moves between devices by JAX's collectives and lax.ppermute only.
A program may use at most 64 MiB of HBM per device.

v0:
```python
import jax
import jax.numpy as jnp
from jax import lax
from jax.experimental import pallas as pl
from jax.experimental.pallas import tpu as pltpu
from jax.sharding import PartitionSpec as P

BS = 128
ITERS = 2
NB = 32
CAP = 4
NS = NB * CAP
ROUNDS = 8
ZERO = 2 * NS
S_CAP = 104
D_CAP = 80
E_CAP = NB
PAIRS = 256
UNROLL = 4
MANY = 4
LIST = 2 * PAIRS + 2 * UNROLL + 8
NZ, NC = 8, 2
NX, NY = 4, 4
SHARD = CAP * BS // 8
PART = SHARD // NC
UNIT = NZ * NC * PART
PANEL = 4 * UNIT
RAW_HALF = 4 * PANEL
WIDE = 40
WORD = 4096
F32 = jnp.float32
BF16 = jnp.bfloat16


def panel_cols(tile, layers):
    row_count, shard_cols = tile.shape
    gathered = lax.all_gather(tile, "row", axis=0, tiled=True)
    pieces = gathered.reshape(
        gathered.shape[0] // (shard_cols * layers), layers, shard_cols, shard_cols
    )
    arranged = lax.all_to_all(pieces, "layer", split_axis=1, concat_axis=3, tiled=True)
    return arranged.reshape(-1, layers * shard_cols)


def multiply(left_tile, right_panel):
    partial_sum = jnp.dot(
        lax.all_gather(left_tile, "col", axis=1, tiled=True),
        right_panel,
        precision=lax.Precision.HIGHEST,
        preferred_element_type=jnp.float32,
    )
    return lax.psum_scatter(partial_sum, "layer", scatter_dimension=1, tiled=True)


def dense_plan(density, pattern):
    row_index = lax.axis_index("row")
    col_index = lax.axis_index("col")
    layer_index = lax.axis_index("layer")
    layers = lax.axis_size("layer")
    row_count, shard_cols = density.shape
    blocks = pattern.shape[0]
    block_line = jnp.arange(blocks, dtype=jnp.int32)
    row_ids = (row_index * row_count + jnp.arange(row_count, dtype=jnp.int32)) // BS
    col_ids = (
        (col_index * layers + layer_index) * shard_cols + jnp.arange(shard_cols, dtype=jnp.int32)
    ) // BS
    pick_rows = (row_ids[:, None] == block_line[None, :]).astype(jnp.float32)
    pick_cols = (col_ids[:, None] == block_line[None, :]).astype(jnp.float32)
    occupied = pattern.astype(jnp.float32)
    in_pattern = jnp.dot(
        jnp.dot(pick_rows, occupied, precision=lax.Precision.HIGHEST),
        pick_cols.T,
        precision=lax.Precision.HIGHEST,
    )
    current = in_pattern * density
    for iteration in range(ITERS):
        current_panel = panel_cols(current, layers)
        squared = in_pattern * multiply(current, current_panel)
        cube_term = in_pattern * multiply(current, panel_cols(squared, layers))
        current = 3.0 * squared - 2.0 * cube_term
    return current


def here():
    row = lax.axis_index("row").astype(jnp.int32)
    column = lax.axis_index("col") * lax.axis_size("layer") + lax.axis_index("layer")
    return row, column.astype(jnp.int32)


def ring_place(source, at):
    back = (at - source) & 3
    return jnp.where(back == 3, 2, jnp.where(back == 2, 3, back))


def raw_row(column, p, h, j, r):
    px = ring_place((column & 1) * 2 + (p >> 2), (j & 1) * 2 + (r >> 2))
    py = ring_place(p & 3, r & 3)
    near, far = ((px, py), (py, px))[h]
    other = jnp.where(((j >> 1) & 1) == h, 0, 1)
    high = near >> 1
    group = jnp.where(far == 0, high, jnp.where(far == 3, 6 + high, 1 + 2 * high + far))
    return other * RAW_HALF + group * (PANEL // 2) + (near & 1) * UNIT + (column >> 1) * PART


def pack_kernel(pat_ref, tile_ref, packed_ref, own_ref, own_t_ref, rank_ref):
    r, j = here()
    K = (pat_ref[...] != 0).astype(F32)
    ii = lax.broadcasted_iota(jnp.int32, (NB, NB), 0)
    jj = lax.broadcasted_iota(jnp.int32, (NB, NB), 1)
    diag = (ii == jj).astype(F32)
    left = K * (1.0 - diag)
    own = diag
    own_t = diag
    after = (ii > jj).astype(F32)
    before = (ii < jj).astype(F32)
    for _ in range(ROUNDS):
        fc = (jnp.sum(left, axis=0, keepdims=True) <= CAP - 1).astype(F32)
        fr = (jnp.sum(left, axis=1, keepdims=True) <= CAP - 1).astype(F32)
        own = own + left * fc * ((1.0 - fr) + fr * after)
        own_t = own_t + left * fr * ((1.0 - fc) + fc * before)
        left = left * (1.0 - fc) * (1.0 - fr)
    own = own + left * after
    own_t = own_t + left * before
    rank = jnp.dot(after, own, preferred_element_type=F32)
    own_ref[...] = own
    own_t_ref[...] = own_t
    rank_ref[...] = rank

    for s in range(CAP):
        total = jnp.zeros((BS, BS), F32)
        for a in range(tile_ref.shape[0] // BS):
            at = (ii == r * (tile_ref.shape[0] // BS) + a) & (jj == j)
            pick = at & (own > 0) & (rank == s)
            w = jnp.sum(jnp.where(pick, 1.0, 0.0), axis=(0, 1), keepdims=True)
            total = total + w * tile_ref[a * BS : (a + 1) * BS, :]
        packed_ref[s * BS : (s + 1) * BS, :] = total


def plan_kernel(
    pat_ref, own_ref, own_t_ref, rank_ref,
    cid_ref, nbr_ref, deg_ref, needed_ref, count_ref, rows_a, rows_b, ok_ref,
):
    r, j = here()
    K = (pat_ref[...] != 0).astype(F32)
    ii = lax.broadcasted_iota(jnp.int32, (NB, NB), 0)
    jj = lax.broadcasted_iota(jnp.int32, (NB, NB), 1)
    before = (ii < jj).astype(F32)
    own = own_ref[...]
    own_t = own_t_ref[...]
    rank = rank_ref[...]
    rank_t = jnp.dot(own_t, before, preferred_element_type=F32)
    slot = jj * CAP + rank.astype(jnp.int32)
    slot_t = ii * CAP + rank_t.astype(jnp.int32)
    cid = jnp.where(own > 0, slot, jnp.where(own_t > 0, NS + slot_t, ZERO))
    cid_ref[...] = jnp.full(cid_ref.shape, ZERO, jnp.int32)
    cid_ref[:NB, :] = cid
    column = jnp.where(own > 0, jj, ii)
    turn = jnp.where(own > 0, rank, rank_t).astype(jnp.int32)
    for n, row_ref in enumerate((rows_a, rows_b)):
        first, second = [raw_row(column, 2 * turn + n, h, j, r) // PART for h in range(2)]
        row_ref[...] = first + second * WORD

    common = jnp.dot(K, K, preferred_element_type=F32)
    pairs = K * jnp.floor((common + 1.0) * 0.5)
    s_blocks = jnp.max(jnp.sum(common, axis=1))
    d_blocks = jnp.max(jnp.sum(common * K, axis=1))
    spread = jnp.dot(K, pairs, preferred_element_type=F32)
    s_pairs = jnp.max(jnp.sum(spread, axis=1))
    fits = (
        (jnp.max(jnp.sum(own, axis=0)) <= CAP)
        & (s_blocks <= S_CAP)
        & (d_blocks <= D_CAP)
        & (s_pairs <= PAIRS)
    )
    ok_ref[0] = fits.astype(jnp.int32)

    kj = jnp.sum(jnp.where(jj == j, K, 0.0), axis=1, keepdims=True)
    near = lax.dot_general(K * kj, K, (((0,), (0,)), ((), ())), preferred_element_type=F32)
    wanted = jnp.where((near > 0) & (K > 0), 1.0, 0.0)
    wide = lax.broadcasted_iota(jnp.int32, (NB, WIDE), 1)
    for listed, n_ref, entries in (
        (K, deg_ref, ((jj + cid * WORD, NB + ZERO * WORD, nbr_ref),)),
        (wanted, count_ref, ((jj, NB, needed_ref),)),
    ):
        place = jnp.dot(listed, before, preferred_element_type=F32).astype(jnp.int32)
        place = jnp.where(listed > 0, place, -1)
        size = jnp.sum(listed, axis=1, keepdims=True).astype(jnp.int32)
        for value, empty, list_ref in entries:
            out = jnp.full((NB, WIDE), empty, jnp.int32)
            for d in range(NB):
                entry = jnp.sum(jnp.where(place == d, value, 0), axis=1, keepdims=True)
                out = jnp.where((wide == d) & (size > d), entry, out)
            list_ref[...] = out
        n_ref[...] = jnp.broadcast_to(size, (NB, NB))


H_S, H_T, H_E, H_F, H_SB, H_DB, H_EB = range(7)


def block_kernel(ok_ref, cid, needed, count_in, rows_a, rows_b, head_ref, pn_ref, pt_ref, an_ref, at_ref):
    ok = ok_ref[0]

    def lines(i, carry):
        def entry(d, c):
            pn, pt = c
            k = needed[i, d]
            held = cid[i, k]
            rows = (rows_a[i, k], rows_b[i, k])
            flipped = (held >= NS).astype(jnp.int32)
            pn_ref[pn] = held
            pt_ref[pt] = held
            for n, row in enumerate(rows):
                an_ref[2 * pn + n] = row
                at_ref[2 * pt + n] = row
            return pn + (1 - flipped), pt + flipped

        return lax.fori_loop(0, count_in[i, 0] * ok, entry, carry)

    pn, pt = lax.fori_loop(0, NB, lines, (0, 0))
    for names, rows, n in ((pn_ref, an_ref, pn), (pt_ref, at_ref, pt)):
        for u in range(MANY - 1):
            names[n + u] = ZERO + 1
            for part in range(2):
                rows[2 * (n + u) + part] = 0
    head_ref[0] = pn
    head_ref[1] = pt


def table_kernel(
    ok_ref, cid, nbr, deg_in,
    head_ref, sl, sr, tt, el, er, fl, fr, ds_ref, fin_ref,
    did, eid,
):
    r, j = here()
    ok = ok_ref[0]
    nj = deg_in[j, 0] * ok

    def row(a, carry):
        m = nbr[j, a] & (WORD - 1)
        nm = deg_in[m, 0]
        base = carry[1] * WORD

        def output(b, c):
            pos, count, dcount, tcount = c
            k = nbr[m, b] & (WORD - 1)
            out = count * WORD

            def four(g, p):
                at = g * 4
                words = [nbr[m, at + u] for u in range(4)]
                rs = [cid[w & (WORD - 1), k] for w in words]
                for u in range(4):
                    sl[p] = (words[u] >> 12) + (base + (at + u) * WORD)
                    sr[p] = rs[u] + out
                    p = p + (rs[u] != ZERO).astype(jnp.int32)
                return p

            p = lax.fori_loop(0, (nm + 3) >> 2, four, pos)
            sl[p] = ZERO + S_CAP * WORD
            sr[p] = ZERO + out
            p = p + (p & 1)

            def reuse(pair, t):
                tt[t] = pair + dcount * WORD
                return t + 1

            inside = (cid[k, j] != ZERO).astype(jnp.int32)
            first = pos >> 1
            tcount = lax.fori_loop(first, first + inside * ((p >> 1) - first), reuse, tcount)
            did[m, k] = dcount
            ds_ref[dcount] = count
            return p, count + 1, dcount + inside, tcount

        return lax.fori_loop(0, nm, output, carry)

    pos, count, dcount, tcount = lax.fori_loop(0, nj, row, (0, 0, 0, 0))
    for t in range(2 * UNROLL):
        sl[pos + t] = ZERO + S_CAP * WORD
        sr[pos + t] = ZERO + S_CAP * WORD
    for t in range(UNROLL):
        tt[tcount + t] = (pos >> 1) + D_CAP * WORD
    for u in range(MANY - 1):
        ds_ref[dcount + u] = 0
    head_ref[H_S] = ((pos >> 1) + UNROLL - 1) // UNROLL
    head_ref[H_T] = (tcount + UNROLL - 1) // UNROLL
    head_ref[H_SB] = count
    head_ref[H_DB] = dcount

    def finish(refs, pos, lz, dummy):
        L, R = refs
        for t in range(2 * UNROLL):
            L[pos + t] = lz
            R[pos + t] = D_CAP + dummy * WORD
        return ((pos >> 1) + UNROLL - 1) // UNROLL

    def gather(refs, pos, k, left, out, lz):
        L, R = refs

        def entry(c, p):
            m = nbr[j, c] & (WORD - 1)
            L[p] = left(m)
            R[p] = did[m, k] + out * WORD
            return p + (cid[m, k] != ZERO).astype(jnp.int32)

        p = lax.fori_loop(0, nj, entry, pos)
        L[p] = lz
        R[p] = D_CAP + out * WORD
        return p + (p & 1)

    def e_out(b, pos):
        k = nbr[j, b] & (WORD - 1)
        eid[k] = b
        return gather((el, er), pos, k, lambda m: did[j, m], b, D_CAP)

    pos = lax.fori_loop(0, nj, e_out, 0)
    head_ref[H_E] = finish((el, er), pos, D_CAP, E_CAP)
    head_ref[H_EB] = nj

    per = NB // 8

    def f_out(a, pos):
        i = r * per + a

        def stored(pos):
            fin_ref[a] = eid[i]
            return gather((fl, fr), pos, i, lambda k: eid[k], a, E_CAP)

        def absent(pos):
            fin_ref[a] = -1
            return pos

        return lax.cond((cid[i, j] != ZERO) & (ok != 0), stored, absent, pos)

    pos = lax.fori_loop(0, per, f_out, 0)
    head_ref[H_F] = finish((fl, fr), pos, E_CAP, per)


def split(x):
    hi = x.astype(BF16)
    return hi, (x - hi.astype(F32)).astype(BF16)


def compute_kernel(
    blocks_ref, pn_ref, pt_ref, an_ref, at_ref, head_ref, sl, sr, tt, el, er, fl, fr, ds_ref, fin_ref,
    *rest,
):
    pieces, rest = rest[:-15], rest[-15:]
    out_ref, raw, ch, cl, sa, sh, slo, da, dh, dl, ea, eh, elo, fa, sem = rest
    copies = []
    row = 0
    for n, piece in enumerate(pieces):
        height = piece.shape[0]
        copies.append(pltpu.make_async_copy(piece, raw.at[pl.ds(row, height)], sem.at[n]))
        row += height
    for c in copies:
        c.start()
    zero = jnp.zeros((BS, BS), BF16)
    for hi, lo, at in ((ch, cl, ZERO), (sh, slo, S_CAP), (dh, dl, D_CAP), (eh, elo, E_CAP)):
        hi[at] = zero
        lo[at] = zero

    def clear(ref, n):
        @pl.loop(0, n)
        def _(t):
            ref[t] = jnp.zeros((BS, BS), F32)

    clear(sa, head_ref[H_SB])
    clear(da, head_ref[H_DB])
    clear(ea, head_ref[H_EB])
    clear(fa, fa.shape[0])
    for c in copies:
        c.wait()

    def prepare(n, names, rows, turn):
        @pl.loop(0, (n + MANY - 1) // MANY)
        def _(t):
            ids = [names[MANY * t + u] for u in range(MANY)]
            xs = []
            for u in range(MANY):
                words = [rows[2 * (MANY * t + u) + n] for n in range(2)]
                starts = [w & (WORD - 1) if h == 0 else w >> 12 for w in words for h in range(2)]
                parts = [raw[pl.ds(pl.multiple_of(at * PART, PART), PART), :] for at in starts]
                xs.append(split(turn(jnp.concatenate(parts, axis=0))))
            for a, (hi, lo) in zip(ids, xs):
                ch[a] = hi
                cl[a] = lo

    prepare(blocks_ref[0], pn_ref, an_ref, lambda v: v)
    prepare(blocks_ref[1], pt_ref, at_ref, lambda v: v.T)

    def phase(n, task, left, right, acc):
        lh, ll = left
        rh, rl = right

        @pl.loop(0, n)
        def _(t):
            sums = []
            outs = []
            for u in range(UNROLL):
                a0, a1, b0, b1, out = task(t * UNROLL + u)
                lhs = jnp.concatenate(
                    [
                        jnp.concatenate([lh[a0], lh[a1]], axis=1),
                        jnp.concatenate([ll[a0], ll[a1]], axis=1),
                    ],
                    axis=0,
                )
                rhs = jnp.concatenate(
                    [
                        jnp.concatenate([rh[b0], rl[b0]], axis=1),
                        jnp.concatenate([rh[b1], rl[b1]], axis=1),
                    ],
                    axis=0,
                )
                both = jnp.dot(lhs, rhs, preferred_element_type=F32)
                sums.append(both[:BS, :BS] + (both[:BS, BS:] + both[BS:, :BS]))
                outs.append(out)
            for u in range(UNROLL):
                acc[outs[u]] = acc[outs[u]] + sums[u]

    def plain(L, R):
        def task(t):
            r0 = R[2 * t]
            low = lambda w: w & (WORD - 1)
            return low(L[2 * t]), low(L[2 * t + 1]), low(r0), low(R[2 * t + 1]), r0 >> 12

        return task

    def cube(t):
        word = tt[t]
        at = 2 * (word & (WORD - 1))
        return sl[at] >> 12, sl[at + 1] >> 12, sr[at] & (WORD - 1), sr[at + 1] & (WORD - 1), word >> 12

    phase(head_ref[H_S], plain(sl, sr), (ch, cl), (ch, cl), sa)

    @pl.loop(0, (head_ref[H_SB] + MANY - 1) // MANY)
    def _(t):
        done = [split(sa[MANY * t + u]) for u in range(MANY)]
        for u in range(MANY):
            sh[MANY * t + u], slo[MANY * t + u] = done[u]

    phase(head_ref[H_T], cube, (sh, slo), (ch, cl), da)

    @pl.loop(0, (head_ref[H_DB] + MANY - 1) // MANY)
    def _(t):
        done = [split(3.0 * sa[ds_ref[MANY * t + u]] - 2.0 * da[MANY * t + u]) for u in range(MANY)]
        for u in range(MANY):
            dh[MANY * t + u], dl[MANY * t + u] = done[u]

    phase(head_ref[H_E], plain(el, er), (dh, dl), (dh, dl), ea)

    @pl.loop(0, head_ref[H_EB])
    def _(t):
        eh[t], elo[t] = split(ea[t])

    phase(head_ref[H_F], plain(fl, fr), (eh, elo), (dh, dl), fa)
    for a in range(out_ref.shape[0] // BS):
        at = fin_ref[a]
        value = 3.0 * ea[jnp.maximum(at, 0)] - 2.0 * fa[a]
        out_ref[a * BS : (a + 1) * BS, :] = jnp.where(at >= 0, value.T, 0.0)


def linear(x, y, z, core):
    return (((x % 2) * NY + y) * (NZ * NC) + z * NC + core) * 2 + x // 2


def send(value, step):
    pairs = [
        (linear(x, y, z, core), linear(*step(x, y, z, core)))
        for x in range(NX)
        for y in range(NY)
        for z in range(NZ)
        for core in range(NC)
    ]
    return lax.ppermute(value, ("row", "col", "layer"), pairs)


def along_z(d):
    return lambda x, y, z, core: (x, y, (z + d) % NZ, core)


def inner(d):
    return lambda x, y, z, core: ((x + d) % NX, y, z, core) if core == 0 else (x, (y + d) % NY, z, core)


def outer(d):
    return lambda x, y, z, core: (x, (y + d) % NY, z, core) if core == 0 else ((x + d) % NX, y, z, core)


def other_core(x, y, z, core):
    return x, y, z, 1 - core


def list_blocks(ok, *plan):
    smem = pl.BlockSpec(memory_space=pltpu.SMEM)
    i32 = lambda *shape: jax.ShapeDtypeStruct(shape, jnp.int32)
    return pl.pallas_call(
        block_kernel,
        out_shape=[i32(8), *[i32(2 * NS + 8)] * 2, *[i32(4 * NS + 16)] * 2],
        in_specs=[smem] * 6,
        out_specs=[smem] * 5,
        cost_estimate=pl.CostEstimate(flops=0, bytes_accessed=6_000_000, transcendentals=0),
        name="list_blocks",
    )(ok, *plan)


def list_products(ok, *plan):
    smem = pl.BlockSpec(memory_space=pltpu.SMEM)
    i32 = lambda *shape: jax.ShapeDtypeStruct(shape, jnp.int32)
    return pl.pallas_call(
        table_kernel,
        out_shape=[i32(16), *[i32(LIST)] * 7, i32(D_CAP + MANY), i32(8)],
        in_specs=[smem] * 4,
        out_specs=[smem] * 10,
        scratch_shapes=[
            pltpu.SMEM((NB, NB), jnp.int32),
            pltpu.SMEM((NB,), jnp.int32),
        ],
        cost_estimate=pl.CostEstimate(flops=0, bytes_accessed=20_000_000, transcendentals=0),
        name="list_products",
    )(ok, *plan)


def plan_products(pattern, *owners):
    smem = pl.BlockSpec(memory_space=pltpu.SMEM)
    vmem = pl.BlockSpec(memory_space=pltpu.VMEM)
    i32 = lambda *shape: jax.ShapeDtypeStruct(shape, jnp.int32)
    return pl.pallas_call(
        plan_kernel,
        out_shape=(
            i32(WIDE, NB), i32(NB, WIDE), i32(NB, NB), i32(NB, WIDE), i32(NB, NB),
            *[i32(NB, NB)] * 2,
            i32(1),
        ),
        in_specs=[vmem] * 4,
        out_specs=(*[vmem] * 7, smem),
        cost_estimate=pl.CostEstimate(flops=0, bytes_accessed=10_000_000, transcendentals=0),
        name="plan_products",
    )(pattern, *owners)


def to_chips_along_z(shard):
    parts = jnp.broadcast_to(shard.reshape(NC, PART, BS), (NZ, NC, PART, BS)).reshape(NZ * NC, PART, BS)
    return lax.all_to_all(parts, "col", split_axis=0, concat_axis=0, tiled=True).reshape(UNIT, BS)


def gather_pieces(shard, pattern, owners):
    tie = lax.optimization_barrier
    swap = lambda value: send(value, other_core)
    own = to_chips_along_z(shard)
    back, ahead, opposite = [send(own, inner(d)) for d in (1, -1, 2)]

    back, owners = tie((back, owners))
    low = jnp.concatenate([own, back], axis=0)
    back_low, ahead_low = send(low, outer(1)), send(low, outer(-1))
    their_low = swap(low)
    cid, nbr, deg, needed, count, rows_a, rows_b, ok = plan_products(pattern, *owners)
    blocks = list_blocks(ok, cid, needed, count, rows_a, rows_b)
    ahead, opposite, blocks = tie((ahead, opposite, blocks))

    high = jnp.concatenate([ahead, opposite], axis=0)
    back_high, ahead_high = send(high, outer(1)), send(high, outer(-1))
    their_high = swap(high)
    back_low, ahead_low, cid = tie((back_low, ahead_low, cid))
    far_low = send(back_low, outer(1))
    middle = [swap(back_low), swap(ahead_low)]
    tables = list_products(ok, cid, nbr, deg)
    back_high, ahead_high, far_low, tables = tie((back_high, ahead_high, far_low, tables))
    far_high = send(ahead_high, outer(-1))
    last = [swap(back_high), swap(ahead_high), swap(far_low)]
    far_high = tie(far_high)
    mine = [low, high, back_low, ahead_low, back_high, ahead_high, far_low, far_high]
    return ok, [*blocks, *tables], [*mine, their_low, their_high, *middle, *last, swap(far_high)]


def per_device(density, pattern):
    smem = pl.BlockSpec(memory_space=pltpu.SMEM)
    vmem = pl.BlockSpec(memory_space=pltpu.VMEM)

    square = jax.ShapeDtypeStruct((NB, NB), F32)
    packed, *owners = pl.pallas_call(
        pack_kernel,
        out_shape=(jax.ShapeDtypeStruct((CAP * BS, BS), F32), square, square, square),
        in_specs=[vmem, vmem],
        out_specs=[vmem] * 4,
        name="pack_blocks",
    )(pattern, density)

    rows = lax.axis_size("row")
    pieces = packed.reshape(rows, SHARD, BS)
    shard = jnp.sum(lax.all_to_all(pieces, "row", split_axis=0, concat_axis=0, tiled=True), axis=0)
    ok, tables, gathered = gather_pieces(shard, pattern, owners)

    def sparse(density, pattern, tables, gathered):
        block = lambda n, t: pltpu.VMEM((n, BS, BS), t)
        return pl.pallas_call(
            compute_kernel,
            out_shape=jax.ShapeDtypeStruct(density.shape, F32),
            in_specs=[smem] * len(tables) + [pl.BlockSpec(memory_space=pl.ANY)] * len(gathered),
            out_specs=vmem,
            scratch_shapes=[
                pltpu.VMEM((2 * RAW_HALF, BS), F32),
                block(ZERO + 2, BF16), block(ZERO + 2, BF16),
                block(S_CAP + 1, F32), block(S_CAP + 1, BF16), block(S_CAP + 1, BF16),
                block(D_CAP + 1, F32), block(D_CAP + 1, BF16), block(D_CAP + 1, BF16),
                block(E_CAP + 1, F32), block(E_CAP + 1, BF16), block(E_CAP + 1, BF16),
                block(NB // 8 + 1, F32),
                pltpu.SemaphoreType.DMA((len(gathered),)),
            ],
            compiler_params=pltpu.CompilerParams(vmem_limit_bytes=60 * 2**20),
            name="purify_column",
        )(*tables, *gathered)

    def dense(density, pattern, tables, gathered):
        return dense_plan(density, pattern)

    return lax.cond(ok[0] != 0, sparse, dense, density, pattern, tables, gathered)


def solution(mesh):
    return jax.shard_map(
        per_device,
        mesh=mesh,
        in_specs=(P("row", ("col", "layer")), P()),
        out_specs=P("row", ("col", "layer")),
        check_vma=False,
    )
```

profile of v0, /device:TPU:1, one launch (start us, length us, event | category | flops | bytes accessed | tf_op | source)
XLA Modules:
  0.0 114.2 jit_solution(10177567220374567602)
XLA Ops:
  6.5 0.0 copy-start.9
  6.5 0.0 copy-start.4
  6.5 2.7 %pack_blocks.1 = (f32[512,128]{1,0:T(8,128)}, f32[32,32]{1,0:T(8,128)}, f32[32,32]{1,0:T(8,128)}, f32[32,32]{1,0:T(8,128)}) custom-call(s32[32,32]{1,0:T(8,128)} %pat_ref.3, f32[512,128]{1,0:T(8,128)} %tile_ref.1), custom_call_target="tpu_custom_call" | custom-call | tf_op jit(solution)/shard_map/pack_blocks/pallas_call | solution.py:581
  9.2 12.1 %all_to_all.62 = f32[8,64,128]{2,1,0:T(8,128)S(1)} all-to-all(f32[8,64,128]{2,1,0:T(8,128)} %bitcast.67), channel_id=1, replica_groups=mesh['row'=8,'col'=16,'layer'=2] {'row'}, dimensions={0} | all-to-all | bytes 524288 | tf_op jit(solution)/shard_map/all_to_all | solution.py:591
  21.3 22.1 %all_to_all.63 = f32[16,32,128]{2,1,0:T(8,128)S(1)} all-to-all(f32[16,32,128]{2,1,0:T(8,128)S(1)} %bitcast.62), channel_id=1, replica_groups=mesh['row'=8,'col'=16,'layer'=2] {'col'}, dimensions={0} | all-to-all | bytes 524288 | tf_op jit(solution)/shard_map/all_to_all | solution.py:544
  43.4 0.0 collective-permute-start
  43.4 6.7 %collective-permute-done = f32[512,128]{1,0:T(8,128)S(1)} collective-permute-done((f32[512,128]{1,0:T(8,128)S(1)}, f32[512,128]{1,0:T(8,128)S(1)}, u32[]{:S(2)}, u32[]{:S(2)}) %collective-permute-start) | collective-permute-done | bytes 262176 | tf_op jit(solution)/shard_map/ppermute | solution.py:475
  50.2 1.4 %collective-permute-start.6 = (f32[1024,128]{1,0:T(8,128)S(1)}, f32[1024,128]{1,0:T(8,128)S(1)}, u32[]{:S(2)}, u32[]{:S(2)}) collective-permute-start(f32[1024,128]{1,0:T(8,128)S(1)} %pad_maximum_fusion), channel_id=1, source_target_pairs={{0,96},{2,131},{4,100},{6,135},{8,104},{10,139},{12,108},{14,143},... | collective-permute-start | bytes 1572872 | tf_op jit(solution)/shard_map/ppermute | solution.py:475
  51.6 0.1 collective-permute-start.5
  51.7 0.0 collective-permute-start.2
  51.7 1.9 %collective-permute-start.1 = (f32[512,128]{1,0:T(8,128)S(1)}, f32[512,128]{1,0:T(8,128)S(1)}, u32[]{:S(2)}, u32[]{:S(2)}) collective-permute-start(f32[512,128]{1,0:T(8,128)S(1)} %bitcast.66), channel_id=1, source_target_pairs={{0,129},{2,98},{4,133},{6,102},{8,137},{10,106},{12,141},{14,110},... | collective-permute-start | bytes 786440 | tf_op jit(solution)/shard_map/ppermute | solution.py:475
  53.6 0.0 copy-done.9
  53.6 2.3 %plan_products.1 = (s32[40,32]{1,0:T(8,128)}, s32[32,40]{1,0:T(8,128)}, s32[32,32]{1,0:T(8,128)}, s32[32,40]{1,0:T(8,128)}, s32[32,32]{1,0:T(8,128)}, /*index=5*...) custom-call(s32[32,32]{1,0:T(8,128)S(1)} %copy-done.9, f32[32,32]{1,0:T(8,128)} %get-tuple-element.165.own_ref, ...), custom_call_target="tpu_custom_call" | custom-call | bytes 10000000 | tf_op jit(solution)/shard_map/plan_products/pallas_call | solution.py:528
  55.9 4.6 %list_blocks.1 = (s32[8]{0:T(128)S(1)}, s32[264]{0:T(512)S(1)}, s32[264]{0:T(512)S(1)}, s32[528]{0:T(1024)S(1)}, s32[528]{0:T(1024)S(1)}) custom-call(s32[1]{0:T(128)} %get-tuple-element.168.ok_ref, s32[40,32]{1,0:T(8,128)} %get-tuple-element.188.cid, s32[32,40]{1,0:T(8,128)} %get-tuple-element.170.needed, s32[32,32]{1,0:T(8,128)} %get-tuple-element.171.count_in, ...), custom_call_target="tpu_custom_call" | custom-call | bytes 6000000 | tf_op jit(solution)/shard_map/list_blocks/pallas_call | solution.py:497
  60.5 1.1 collective-permute-done.2
  61.6 3.1 %collective-permute-done.1 = f32[512,128]{1,0:T(8,128)S(1)} collective-permute-done((f32[512,128]{1,0:T(8,128)S(1)}, f32[512,128]{1,0:T(8,128)S(1)}, u32[]{:S(2)}, u32[]{:S(2)}) %collective-permute-start.1) | collective-permute-done | bytes 262176 | tf_op jit(solution)/shard_map/ppermute | solution.py:475
  64.7 0.9 collective-permute-start.4
  65.6 0.7 collective-permute-start.3
  66.3 0.0 collective-permute-done.6
  66.3 0.0 collective-permute-done.5
  66.3 0.1 collective-permute-start.7
  66.4 6.5 %list_products.1 = (s32[16]{0:T(128)S(1)}, s32[528]{0:T(1024)S(1)}, s32[528]{0:T(1024)S(1)}, s32[528]{0:T(1024)S(1)}, s32[528]{0:T(1024)S(1)}, /*index=5*/s32[52...) custom-call(s32[1]{0:T(128)} %get-tuple-element.168.ok_ref, ...), custom_call_target="tpu_custom_call" | custom-call | bytes 20000000 | tf_op jit(solution)/shard_map/list_products/pallas_call | solution.py:510
  72.8 0.4 collective-permute-done.4
  73.2 2.0 %collective-permute-done.3 = f32[1024,128]{1,0:T(8,128)} collective-permute-done((f32[1024,128]{1,0:T(8,128)S(1)}, f32[1024,128]{1,0:T(8,128)}, u32[]{:S(2)}, u32[]{:S(2)}) %collective-permute-start.3) | collective-permute-done | bytes 524320 | tf_op jit(solution)/shard_map/ppermute | solution.py:475
  75.2 5.3 %collective-permute-done.7 = f32[1024,128]{1,0:T(8,128)} collective-permute-done((f32[1024,128]{1,0:T(8,128)S(1)}, f32[1024,128]{1,0:T(8,128)}, u32[]{:S(2)}, u32[]{:S(2)}) %collective-permute-start.7) | collective-permute-done | bytes 524320 | tf_op jit(solution)/shard_map/ppermute | solution.py:475
  80.6 0.2 collective-permute-start.8
  80.8 0.1 collective-permute-start.10
  80.9 0.4 collective-permute-start.9
  81.3 0.1 collective-permute-start.12
  81.4 0.4 collective-permute-start.11
  81.8 7.2 %collective-permute-done.8 = f32[1024,128]{1,0:T(8,128)} collective-permute-done((f32[1024,128]{1,0:T(8,128)S(1)}, f32[1024,128]{1,0:T(8,128)}, u32[]{:S(2)}, u32[]{:S(2)}) %collective-permute-start.8) | collective-permute-done | bytes 524320 | tf_op jit(solution)/shard_map/ppermute | solution.py:475
  89.0 1.2 %collective-permute-start.14 = (f32[1024,128]{1,0:T(8,128)S(1)}, f32[1024,128]{1,0:T(8,128)}, u32[]{:S(2)}, u32[]{:S(2)}) collective-permute-start(f32[1024,128]{1,0:T(8,128)S(1)} %collective-permute-done.4), channel_id=1, source_target_pairs={{0,2},{2,0},{4,6},{6,4},{8,10},{10,8},{12,14},{14,12},{16,18},{18,... | collective-permute-start | bytes 1572872 | tf_op jit(solution)/shard_map/ppermute | solution.py:475
  90.2 0.0 collective-permute-done.10
  90.2 0.0 copy-start.5
  90.2 0.1 collective-permute-start.13
  90.3 0.0 collective-permute-done.9
  90.3 0.0 copy-start.6
  90.3 0.4 collective-permute-start.15
  90.7 0.0 collective-permute-done.12
  90.7 0.3 copy-done.5
  91.0 0.0 copy-start.7
  91.0 0.1 collective-permute-start.16
  91.1 0.1 copy-done.6
  91.2 0.6 copy-done.7
  92.5 0.0 collective-permute-done.11
  92.5 0.3 collective-permute-done.13
  92.8 0.7 collective-permute-done.15
  93.6 0.0 collective-permute-done.14
  93.6 0.7 collective-permute-done.16
  94.3 0.0 copy-done.4
  94.3 12.3 %conditional.1 = (f32[512,128]{1,0:T(8,128)S(1)}) conditional(s32[]{:T(128)} %bitcast.16, (s32[32,32]{1,0:T(8,128)S(1)}, f32[512,128]{1,0:T(8,128)S(1)}) %tuple.51, (s32[8]{0:T(128)S(1)}, s32[264]{0:T(512)S(1)}, s32[264]{0:T(512)S(1)}, s32[528]{0:T(1024)S(1)}, s32[528]{0:T(1024)S(1)}, /*index=5*/s32[16]{0:T(128)S(1)}, s32[528]{0:T(1024)S(1)}, ...), branch_computations={%region_1.6_spmd, %region_6.7_spmd} | conditional | flops 12917111808 | bytes 165553760 | solution.py:617
  94.3 12.3 %purify_column.1 = f32[512,128]{1,0:T(8,128)S(1)} custom-call(s32[8]{0:T(128)S(1)} %get-tuple-element.76.blocks_ref, s32[264]{0:T(512)S(1)} %get-tuple-element.77.pn_ref, s32[264]{0:T(512)S(1)} %get-tuple-element.78.pt_ref, s32[528]{0:T(1024)S(1)} %get-tuple-element.79.an_ref, s32[528]{0:T(1024)S(1)} %get-tuple-element.80.at_ref, ...), custom_call_target="tpu_custom_call" | custom-call | tf_op jit(solution)/shard_map/cond/branch_1_fun/purify_column/pallas_call | solution.py:596
  106.7 0.0 copy-start.8
  106.7 0.7 copy-done.8
  (5 shorter events, 0.1 us)
Async XLA Ops:
  6.5 47.1 %copy-start.9 = (s32[32,32]{1,0:T(8,128)S(1)}, s32[32,32]{1,0:T(8,128)}, u32[]{:S(2)}) copy-start(s32[32,32]{1,0:T(8,128)} %pat_ref.3) | copy-start | bytes 12292
  6.5 87.8 %copy-start.4 = (f32[512,128]{1,0:T(8,128)S(1)}, f32[512,128]{1,0:T(8,128)}, u32[]{:S(2)}) copy-start(f32[512,128]{1,0:T(8,128)} %tile_ref.1) | copy-start | bytes 786436
  43.4 6.7 %collective-permute-start = (f32[512,128]{1,0:T(8,128)S(1)}, f32[512,128]{1,0:T(8,128)S(1)}, u32[]{:S(2)}, u32[]{:S(2)}) collective-permute-start(f32[512,128]{1,0:T(8,128)S(1)} %bitcast.63), channel_id=1, source_target_pairs={{0,128},{2,34},{4,132},{6,38},{8,136},{10,42},{12,140},{14,46},{16... | collective-permute-start | bytes 786440 | tf_op jit(solution)/shard_map/ppermute | solution.py:475
  50.2 16.1 %collective-permute-start.6 = (f32[1024,128]{1,0:T(8,128)S(1)}, f32[1024,128]{1,0:T(8,128)S(1)}, u32[]{:S(2)}, u32[]{:S(2)}) collective-permute-start(f32[1024,128]{1,0:T(8,128)S(1)} %pad_maximum_fusion), channel_id=1, source_target_pairs={{0,96},{2,131},{4,100},{6,135},{8,104},{10,139},{12,108},{14,143},... | collective-permute-start | bytes 1572872 | tf_op jit(solution)/shard_map/ppermute | solution.py:475
  51.6 14.7 %collective-permute-start.5 = (f32[1024,128]{1,0:T(8,128)S(1)}, f32[1024,128]{1,0:T(8,128)S(1)}, u32[]{:S(2)}, u32[]{:S(2)}) collective-permute-start(f32[1024,128]{1,0:T(8,128)S(1)} %pad_maximum_fusion), channel_id=1, source_target_pairs={{0,32},{2,130},{4,36},{6,134},{8,40},{10,138},{12,44},{14,142},{16... | collective-permute-start | bytes 1572872 | tf_op jit(solution)/shard_map/ppermute | solution.py:475
  51.7 9.8 %collective-permute-start.2 = (f32[512,128]{1,0:T(8,128)S(1)}, f32[512,128]{1,0:T(8,128)S(1)}, u32[]{:S(2)}, u32[]{:S(2)}) collective-permute-start(f32[512,128]{1,0:T(8,128)S(1)} %bitcast.65), channel_id=1, source_target_pairs={{0,1},{2,66},{4,5},{6,70},{8,9},{10,74},{12,13},{14,78},{16,17},{1... | collective-permute-start | bytes 786440 | tf_op jit(solution)/shard_map/ppermute | solution.py:475
  51.7 13.0 %collective-permute-start.1 = (f32[512,128]{1,0:T(8,128)S(1)}, f32[512,128]{1,0:T(8,128)S(1)}, u32[]{:S(2)}, u32[]{:S(2)}) collective-permute-start(f32[512,128]{1,0:T(8,128)S(1)} %bitcast.66), channel_id=1, source_target_pairs={{0,129},{2,98},{4,133},{6,102},{8,137},{10,106},{12,141},{14,110},... | collective-permute-start | bytes 786440 | tf_op jit(solution)/shard_map/ppermute | solution.py:475
  64.7 8.5 %collective-permute-start.4 = (f32[1024,128]{1,0:T(8,128)S(1)}, f32[1024,128]{1,0:T(8,128)S(1)}, u32[]{:S(2)}, u32[]{:S(2)}) collective-permute-start(f32[1024,128]{1,0:T(8,128)S(1)} %constant_dynamic-update-slice_fusion), channel_id=1, source_target_pairs={{0,96},{2,131},{4,100},{6,135},{8,104},{10,139},{12,108},{14,143},... | collective-permute-start | bytes 1572872 | tf_op jit(solution)/shard_map/ppermute | solution.py:475
  65.6 9.6 %collective-permute-start.3 = (f32[1024,128]{1,0:T(8,128)S(1)}, f32[1024,128]{1,0:T(8,128)}, u32[]{:S(2)}, u32[]{:S(2)}) collective-permute-start(f32[1024,128]{1,0:T(8,128)S(1)} %constant_dynamic-update-slice_fusion), channel_id=1, source_target_pairs={{0,32},{2,130},{4,36},{6,134},{8,40},{10,138},{12,44},{14,142},{16... | collective-permute-start | bytes 1572872 | tf_op jit(solution)/shard_map/ppermute | solution.py:475
  66.3 14.3 %collective-permute-start.7 = (f32[1024,128]{1,0:T(8,128)S(1)}, f32[1024,128]{1,0:T(8,128)}, u32[]{:S(2)}, u32[]{:S(2)}) collective-permute-start(f32[1024,128]{1,0:T(8,128)S(1)} %collective-permute-done.5), channel_id=1, source_target_pairs={{0,32},{2,130},{4,36},{6,134},{8,40},{10,138},{12,44},{14,142},{16... | collective-permute-start | bytes 1572872 | tf_op jit(solution)/shard_map/ppermute | solution.py:475
  80.6 8.4 %collective-permute-start.8 = (f32[1024,128]{1,0:T(8,128)S(1)}, f32[1024,128]{1,0:T(8,128)}, u32[]{:S(2)}, u32[]{:S(2)}) collective-permute-start(f32[1024,128]{1,0:T(8,128)S(1)} %collective-permute-done.4), channel_id=1, source_target_pairs={{0,96},{2,131},{4,100},{6,135},{8,104},{10,139},{12,108},{14,143},... | collective-permute-start | bytes 1572872 | tf_op jit(solution)/shard_map/ppermute | solution.py:475
  80.8 9.4 %collective-permute-start.10 = (f32[1024,128]{1,0:T(8,128)S(1)}, f32[1024,128]{1,0:T(8,128)S(1)}, u32[]{:S(2)}, u32[]{:S(2)}) collective-permute-start(f32[1024,128]{1,0:T(8,128)S(1)} %constant_dynamic-update-slice_fusion), channel_id=1, source_target_pairs={{0,2},{2,0},{4,6},{6,4},{8,10},{10,8},{12,14},{14,12},{16,18},{18,... | collective-permute-start | bytes 1572872 | tf_op jit(solution)/shard_map/ppermute | solution.py:475
  80.9 9.4 %collective-permute-start.9 = (f32[1024,128]{1,0:T(8,128)S(1)}, f32[1024,128]{1,0:T(8,128)S(1)}, u32[]{:S(2)}, u32[]{:S(2)}) collective-permute-start(f32[1024,128]{1,0:T(8,128)S(1)} %pad_maximum_fusion), channel_id=1, source_target_pairs={{0,2},{2,0},{4,6},{6,4},{8,10},{10,8},{12,14},{14,12},{16,18},{18,... | collective-permute-start | bytes 1572872 | tf_op jit(solution)/shard_map/ppermute | solution.py:475
  81.3 9.4 %collective-permute-start.12 = (f32[1024,128]{1,0:T(8,128)S(1)}, f32[1024,128]{1,0:T(8,128)S(1)}, u32[]{:S(2)}, u32[]{:S(2)}) collective-permute-start(f32[1024,128]{1,0:T(8,128)S(1)} %collective-permute-done.6), channel_id=1, source_target_pairs={{0,2},{2,0},{4,6},{6,4},{8,10},{10,8},{12,14},{14,12},{16,18},{18,... | collective-permute-start | bytes 1572872 | tf_op jit(solution)/shard_map/ppermute | solution.py:475
  81.4 11.1 %collective-permute-start.11 = (f32[1024,128]{1,0:T(8,128)S(1)}, f32[1024,128]{1,0:T(8,128)}, u32[]{:S(2)}, u32[]{:S(2)}) collective-permute-start(f32[1024,128]{1,0:T(8,128)S(1)} %collective-permute-done.5), channel_id=1, source_target_pairs={{0,2},{2,0},{4,6},{6,4},{8,10},{10,8},{12,14},{14,12},{16,18},{18,... | collective-permute-start | bytes 1572872 | tf_op jit(solution)/shard_map/ppermute | solution.py:475
  89.0 4.6 %collective-permute-start.14 = (f32[1024,128]{1,0:T(8,128)S(1)}, f32[1024,128]{1,0:T(8,128)}, u32[]{:S(2)}, u32[]{:S(2)}) collective-permute-start(f32[1024,128]{1,0:T(8,128)S(1)} %collective-permute-done.4), channel_id=1, source_target_pairs={{0,2},{2,0},{4,6},{6,4},{8,10},{10,8},{12,14},{14,12},{16,18},{18,... | collective-permute-start | bytes 1572872 | tf_op jit(solution)/shard_map/ppermute | solution.py:475
  90.2 0.8 copy-start.5
  90.2 2.6 %collective-permute-start.13 = (f32[1024,128]{1,0:T(8,128)}, f32[1024,128]{1,0:T(8,128)}, u32[]{:S(2)}, u32[]{:S(2)}) collective-permute-start(f32[1024,128]{1,0:T(8,128)} %collective-permute-done.3), channel_id=1, source_target_pairs={{0,2},{2,0},{4,6},{6,4},{8,10},{10,8},{12,14},{14,12},{16,18},{18,... | collective-permute-start | bytes 1572872 | tf_op jit(solution)/shard_map/ppermute | solution.py:475
  90.3 0.9 copy-start.6
  90.3 3.3 %collective-permute-start.15 = (f32[1024,128]{1,0:T(8,128)}, f32[1024,128]{1,0:T(8,128)}, u32[]{:S(2)}, u32[]{:S(2)}) collective-permute-start(f32[1024,128]{1,0:T(8,128)} %collective-permute-done.7), channel_id=1, source_target_pairs={{0,2},{2,0},{4,6},{6,4},{8,10},{10,8},{12,14},{14,12},{16,18},{18,... | collective-permute-start | bytes 1572872 | tf_op jit(solution)/shard_map/ppermute | solution.py:475
  91.0 0.8 copy-start.7
  91.0 3.3 %collective-permute-start.16 = (f32[1024,128]{1,0:T(8,128)}, f32[1024,128]{1,0:T(8,128)}, u32[]{:S(2)}, u32[]{:S(2)}) collective-permute-start(f32[1024,128]{1,0:T(8,128)} %collective-permute-done.8), channel_id=1, source_target_pairs={{0,2},{2,0},{4,6},{6,4},{8,10},{10,8},{12,14},{14,12},{16,18},{18,... | collective-permute-start | bytes 1572872 | tf_op jit(solution)/shard_map/ppermute | solution.py:475
  106.7 0.7 copy-start.8
where the time goes:
time: 116 us; the launch traced here: 114 us
  blocking collectives  34.1 us (29%)
  Pallas kernels  28.4 us (24%)
  waiting for transfers between devices  27.7 us (24%)
  between operations  14.2 us (12%)
  starting transfers between devices  8.12 us (7%)
  local copies, waits for them, and re-layouts  1.74 us (2%)
    ppermute x17, waiting for transfers between devices, send(): return lax.ppermute(value, ('row', 'col', 'layer'), pairs)  27.7 us
    all_to_all x1, blocking collectives, to_chips_along_z(): lax.all_to_all(parts, 'col', split_axis=0, concat_axis=0, tiled=True)  22.1 us
    pallas_call x1, Pallas kernels, sparse(): pl.pallas_call(compute_kernel, out_shape=jax.ShapeDtypeStruct(density.sha...  12.3 us
    all_to_all x1, blocking collectives, per_device(): lax.all_to_all(pieces, 'row', split_axis=0, concat_axis=0, tiled=True)  12.1 us
    ppermute x17, starting transfers between devices, send(): return lax.ppermute(value, ('row', 'col', 'layer'), pairs)  8.12 us
    pallas_call x1, Pallas kernels, list_products(): pl.pallas_call(table_kernel, out_shape=[i32(16), *[i32(LIST)] * 7, i32(D_...  6.48 us
    pallas_call x1, Pallas kernels, list_blocks(): pl.pallas_call(block_kernel, out_shape=[i32(8), *[i32(2 * NS + 8)] * 2, *...  4.58 us
    pallas_call x1, Pallas kernels, per_device(): pl.pallas_call(pack_kernel, out_shape=(jax.ShapeDtypeStruct((CAP * BS, BS...  2.71 us
  transfers between devices with their start and end apart: 17, of which 10 were waited for; matrix products, arithmetic and copies ran while one was open for 0% of the time, Pallas kernels for 12%

commit v1 on v0

--- a/solution.py
+++ b/solution.py
@@ -98,7 +98,8 @@
     near, far = ((px, py), (py, px))[h]
     other = jnp.where(((j >> 1) & 1) == h, 0, 1)
     high = near >> 1
-    group = jnp.where(far == 0, high, jnp.where(far == 3, 6 + high, 1 + 2 * high + far))
+    ring = 2 + jnp.where(far == 1, 2 * high, 3 - 2 * high)
+    group = jnp.where(far == 0, high, jnp.where(far == 3, 6 + high, ring))
     return other * RAW_HALF + group * (PANEL // 2) + (near & 1) * UNIT + (column >> 1) * PART
 
 
@@ -540,37 +541,41 @@
 
 
 def to_chips_along_z(shard):
-    parts = jnp.broadcast_to(shard.reshape(NC, PART, BS), (NZ, NC, PART, BS)).reshape(NZ * NC, PART, BS)
-    return lax.all_to_all(parts, "col", split_axis=0, concat_axis=0, tiled=True).reshape(UNIT, BS)
+    core = lax.axis_index("col") % NC
+    pick = lambda a, b: jnp.where(core == 0, a, b)
+    halves = shard[:PART], shard[PART:]
+    kept, given = pick(*halves), pick(*halves[::-1])
+    got = send(given, other_core)
+    unit = jnp.concatenate([pick(kept, got), pick(got, kept)], axis=0)
+    lines = [[z * NC + c for z in range(NZ)] for c in range(NC)]
+    copies = jnp.broadcast_to(unit, (NZ, SHARD, BS))
+    return lax.all_to_all(
+        copies, "col", split_axis=0, concat_axis=0, tiled=True, axis_index_groups=lines
+    ).reshape(UNIT, BS)
 
 
 def gather_pieces(shard, pattern, owners):
     tie = lax.optimization_barrier
     swap = lambda value: send(value, other_core)
     own = to_chips_along_z(shard)
-    back, ahead, opposite = [send(own, inner(d)) for d in (1, -1, 2)]
-
-    back, owners = tie((back, owners))
-    low = jnp.concatenate([own, back], axis=0)
-    back_low, ahead_low = send(low, outer(1)), send(low, outer(-1))
-    their_low = swap(low)
+    own, owners = tie((own, owners))
+    line = [own] + [send(own, inner(d)) for d in (1, -1, 2)]
     cid, nbr, deg, needed, count, rows_a, rows_b, ok = plan_products(pattern, *owners)
     blocks = list_blocks(ok, cid, needed, count, rows_a, rows_b)
-    ahead, opposite, blocks = tie((ahead, opposite, blocks))
-
-    high = jnp.concatenate([ahead, opposite], axis=0)
-    back_high, ahead_high = send(high, outer(1)), send(high, outer(-1))
-    their_high = swap(high)
-    back_low, ahead_low, cid = tie((back_low, ahead_low, cid))
-    far_low = send(back_low, outer(1))
-    middle = [swap(back_low), swap(ahead_low)]
+    line, blocks = tie((line, blocks))
+
+    low, high = jnp.concatenate(line[:2], axis=0), jnp.concatenate(line[2:], axis=0)
+    low, high, cid, nbr, deg = tie((low, high, cid, nbr, deg))
+    back_low, ahead_high = send(low, outer(1)), send(high, outer(-1))
+    back_high, ahead_low = send(high, outer(1)), send(low, outer(-1))
     tables = list_products(ok, cid, nbr, deg)
-    back_high, ahead_high, far_low, tables = tie((back_high, ahead_high, far_low, tables))
-    far_high = send(ahead_high, outer(-1))
-    last = [swap(back_high), swap(ahead_high), swap(far_low)]
-    far_high = tie(far_high)
-    mine = [low, high, back_low, ahead_low, back_high, ahead_high, far_low, far_high]
-    return ok, [*blocks, *tables], [*mine, their_low, their_high, *middle, *last, swap(far_high)]
+    back_low, ahead_high, tables = tie((back_low, ahead_high, tables))
+    far_low, far_high = send(back_low, outer(1)), send(ahead_high, outer(-1))
+    theirs = [swap(jnp.concatenate([low, high], axis=0)), swap(back_low), swap(ahead_high)]
+    late = tie([back_high, ahead_low, far_low, far_high])
+    theirs += [swap(value) for value in late]
+    mine = [low, high, back_low, ahead_high, *late]
+    return ok, [*blocks, *tables], [*mine, *theirs]
 
 
 def per_device(density, pattern):

time: 116 us -> 112 us (0.966)
  the two profiles are of different devices: /device:TPU:1 before, /device:TPU:5 now
where the time goes in v1:
time: 112 us; the launch traced here: 114 us
  Pallas kernels  41.5 us (37%)
  starting transfers between devices  20.3 us (18%)
  blocking collectives  19.2 us (17%)
  waiting for transfers between devices  17.7 us (16%)
  between operations  14.1 us (13%)
    pallas_call x1, Pallas kernels, sparse(): pl.pallas_call(compute_kernel, out_shape=jax.ShapeDtypeStruct(density.sha...  21.6 us
    all_to_all x1, blocking collectives, to_chips_along_z(): lax.all_to_all(copies, 'col', split_axis=0, concat_axis=0, tiled=True, ax...  19.2 us
    ppermute x17, starting transfers between devices, send(): return lax.ppermute(value, ('row', 'col', 'layer'), pairs)  15.5 us
    ppermute x17, waiting for transfers between devices, send(): return lax.ppermute(value, ('row', 'col', 'layer'), pairs)  11.6 us
    pallas_call x1, Pallas kernels, list_products(): pl.pallas_call(table_kernel, out_shape=[i32(16), *[i32(LIST)] * 7, i32(D_...  10.1 us
    all_to_all x1, waiting for transfers between devices, per_device(): lax.all_to_all(pieces, 'row', split_axis=0, concat_axis=0, tiled=True)  6.11 us
    pallas_call x1, Pallas kernels, list_blocks(): pl.pallas_call(block_kernel, out_shape=[i32(8), *[i32(2 * NS + 8)] * 2, *...  4.89 us
    all_to_all x1, starting transfers between devices, per_device(): lax.all_to_all(pieces, 'row', split_axis=0, concat_axis=0, tiled=True)  4.83 us
  transfers between devices with their start and end apart: 18, of which 8 were waited for; matrix products, arithmetic and copies ran while one was open for 0% of the time, Pallas kernels for 15%

profile of v1, /device:TPU:5, one launch (start us, length us, event | category | flops | bytes accessed | tf_op | source)
XLA Modules:
  0.0 113.8 jit_solution(17219302886467699830)
XLA Ops:
  6.5 0.0 copy-start.6
  6.5 2.7 %pack_blocks.1 = (f32[512,128]{1,0:T(8,128)}, f32[32,32]{1,0:T(8,128)}, f32[32,32]{1,0:T(8,128)}, f32[32,32]{1,0:T(8,128)}) custom-call(s32[32,32]{1,0:T(8,128)} %pat_ref.3, f32[512,128]{1,0:T(8,128)} %tile_ref.1), custom_call_target="tpu_custom_call" | custom-call | tf_op jit(solution)/shard_map/pack_blocks/pallas_call | solution.py:586
  9.2 4.8 %all-to-all-start.4 = ((f32[8,64,128]{2,1,0:T(8,128)}), f32[8,64,128]{2,1,0:T(8,128)S(1)}, u32[]{:S(2)}, u32[]{:S(2)}) async-start(f32[8,64,128]{2,1,0:T(8,128)} %bitcast.64), calls=%async_computation.8 | async-start | bytes 524288 | tf_op jit(solution)/shard_map/all_to_all | solution.py:596
  14.0 6.1 %all-to-all-done.4 = f32[8,64,128]{2,1,0:T(8,128)S(1)} async-done(((f32[8,64,128]{2,1,0:T(8,128)}), f32[8,64,128]{2,1,0:T(8,128)S(1)}, u32[]{:S(2)}, u32[]{:S(2)}) %all-to-all-start.4) | async-done | bytes 262176 | tf_op jit(solution)/shard_map/all_to_all | solution.py:596
  20.2 2.2 %collective-permute-start = (f32[32,128]{1,0:T(8,128)S(1)}, f32[32,128]{1,0:T(8,128)S(1)}, u32[]{:S(2)}, u32[]{:S(2)}) collective-permute-start(f32[32,128]{1,0:T(8,128)S(1)} %slice_select_fusion), channel_id=1, source_target_pairs={{0,2},{2,0},{4,6},{6,4},{8,10},{10,8},{12,14},{14,12},{16,18},{18,... | collective-permute-start | bytes 49160 | tf_op jit(solution)/shard_map/ppermute | solution.py:476
  22.3 0.8 collective-permute-done
  23.2 19.2 %all_to_all.62 = f32[8,64,128]{2,1,0:T(8,128)S(1)} all-to-all(f32[8,64,128]{2,1,0:T(8,128)S(1)} %broadcast_in_dim.2), channel_id=1, replica_groups={{0,4,8,12,16,20,24,28},{2,6,10,14,18,22,26,30},{1,5,9,13,17,21,25,29},{..., dimensions={0} | all-to-all | bytes 524288 | tf_op jit(solution)/shard_map/all_to_all | solution.py:552
  42.4 0.6 collective-permute-start.3
  43.0 1.7 %collective-permute-start.2 = (f32[512,128]{1,0:T(8,128)S(1)}, f32[512,128]{1,0:T(8,128)S(1)}, u32[]{:S(2)}, u32[]{:S(2)}) collective-permute-start(f32[512,128]{1,0:T(8,128)S(1)} %bitcast.61), channel_id=1, source_target_pairs={{0,129},{2,98},{4,133},{6,102},{8,137},{10,106},{12,141},{14,110},... | collective-permute-start | bytes 786440 | tf_op jit(solution)/shard_map/ppermute | solution.py:476
  44.7 0.0 collective-permute-start.1
  44.7 0.0 copy-done.6
  44.7 2.3 %plan_products.1 = (s32[40,32]{1,0:T(8,128)}, s32[32,40]{1,0:T(8,128)}, s32[32,32]{1,0:T(8,128)}, s32[32,40]{1,0:T(8,128)}, s32[32,32]{1,0:T(8,128)}, /*index=5*...) custom-call(s32[32,32]{1,0:T(8,128)S(1)} %copy-done.6, f32[32,32]{1,0:T(8,128)} %get-tuple-element.169.own_ref, ...), custom_call_target="tpu_custom_call" | custom-call | bytes 10000000 | tf_op jit(solution)/shard_map/plan_products/pallas_call | solution.py:529
  47.0 4.9 %list_blocks.1 = (s32[8]{0:T(128)S(1)}, s32[264]{0:T(512)S(1)}, s32[264]{0:T(512)S(1)}, s32[528]{0:T(1024)S(1)}, s32[528]{0:T(1024)S(1)}) custom-call(s32[1]{0:T(128)} %get-tuple-element.172.ok_ref, s32[40,32]{1,0:T(8,128)} %get-tuple-element.197.cid, s32[32,40]{1,0:T(8,128)} %get-tuple-element.175.needed, s32[32,32]{1,0:T(8,128)} %get-tuple-element.176.count_in, ...), custom_call_target="tpu_custom_call" | custom-call | bytes 6000000 | tf_op jit(solution)/shard_map/list_blocks/pallas_call | solution.py:498
  51.9 0.0 collective-permute-done.3
  51.9 0.0 collective-permute-done.2
  51.9 0.0 collective-permute-done.1
  52.0 0.0 copy-start.4
  52.0 0.1 pad_maximum_fusion.1
  52.0 1.1 collective-permute-start.4
  53.1 0.5 collective-permute-start.5
  53.6 0.1 pad_maximum_fusion
  53.7 4.6 %collective-permute-start.10 = (f32[2048,128]{1,0:T(8,128)S(1)}, f32[2048,128]{1,0:T(8,128)S(1)}, u32[]{:S(2)}, u32[]{:S(2)}) collective-permute-start(f32[2048,128]{1,0:T(8,128)S(1)} %pad_maximum_fusion), channel_id=1, source_target_pairs={{0,2},{2,0},{4,6},{6,4},{8,10},{10,8},{12,14},{14,12},{16,18},{18,... | collective-permute-start | bytes 3145736 | tf_op jit(solution)/shard_map/ppermute | solution.py:476
  58.3 0.3 collective-permute-start.7
  58.6 1.1 %collective-permute-start.6 = (f32[1024,128]{1,0:T(8,128)S(1)}, f32[1024,128]{1,0:T(8,128)}, u32[]{:S(2)}, u32[]{:S(2)}) collective-permute-start(f32[1024,128]{1,0:T(8,128)S(1)} %get-tuple-element.196), channel_id=1, source_target_pairs={{0,32},{2,130},{4,36},{6,134},{8,40},{10,138},{12,44},{14,142},{16... | collective-permute-start | bytes 1572872 | tf_op jit(solution)/shard_map/ppermute | solution.py:476
  59.7 10.1 %list_products.1 = (s32[16]{0:T(128)S(1)}, s32[528]{0:T(1024)S(1)}, s32[528]{0:T(1024)S(1)}, s32[528]{0:T(1024)S(1)}, s32[528]{0:T(1024)S(1)}, /*index=5*/s32[52...) custom-call(s32[1]{0:T(128)} %get-tuple-element.172.ok_ref, ...), custom_call_target="tpu_custom_call" | custom-call | bytes 20000000 | tf_op jit(solution)/shard_map/list_products/pallas_call | solution.py:511
  69.8 0.0 collective-permute-done.4
  69.8 0.0 collective-permute-done.5
  69.8 1.9 %collective-permute-start.8 = (f32[1024,128]{1,0:T(8,128)}, f32[1024,128]{1,0:T(8,128)}, u32[]{:S(2)}, u32[]{:S(2)}) collective-permute-start(f32[1024,128]{1,0:T(8,128)} %collective-permute-done.4), channel_id=1, source_target_pairs={{0,32},{2,130},{4,36},{6,134},{8,40},{10,138},{12,44},{14,142},{16... | collective-permute-start | bytes 1572872 | tf_op jit(solution)/shard_map/ppermute | solution.py:476
  71.7 0.0 collective-permute-start.9
  71.7 0.0 collective-permute-done.7
  71.7 0.0 collective-permute-start.11
  71.7 0.0 collective-permute-done.6
  71.7 0.5 collective-permute-start.12
  72.2 6.0 %collective-permute-done.8 = f32[1024,128]{1,0:T(8,128)} collective-permute-done((f32[1024,128]{1,0:T(8,128)}, f32[1024,128]{1,0:T(8,128)}, u32[]{:S(2)}, u32[]{:S(2)}) %collective-permute-start.8) | collective-permute-done | bytes 524320 | tf_op jit(solution)/shard_map/ppermute | solution.py:476
  78.2 1.8 %collective-permute-done.9 = f32[1024,128]{1,0:T(8,128)} collective-permute-done((f32[1024,128]{1,0:T(8,128)}, f32[1024,128]{1,0:T(8,128)}, u32[]{:S(2)}, u32[]{:S(2)}) %collective-permute-start.9) | collective-permute-done | bytes 524320 | tf_op jit(solution)/shard_map/ppermute | solution.py:476
  80.1 0.0 collective-permute-start.13
  80.1 0.5 collective-permute-start.14
  80.6 0.0 collective-permute-done.10
  80.6 0.0 collective-permute-start.15
  80.6 0.0 collective-permute-done.11
  80.6 0.5 collective-permute-start.16
  81.6 0.0 collective-permute-done.12
  81.7 0.7 collective-permute-done.13
  82.3 0.7 collective-permute-done.14
  83.1 0.7 collective-permute-done.15
  83.8 0.7 collective-permute-done.16
  84.6 0.0 copy-done.4
  84.6 21.6 %conditional.1 = (f32[512,128]{1,0:T(8,128)S(1)}) conditional(s32[]{:T(128)} %bitcast.14, (s32[32,32]{1,0:T(8,128)S(1)}, f32[512,128]{1,0:T(8,128)S(1)}) %tuple.52, (s32[8]{0:T(128)S(1)}, s32[264]{0:T(512)S(1)}, s32[264]{0:T(512)S(1)}, s32[528]{0:T(1024)S(1)}, s32[528]{0:T(1024)S(1)}, /*index=5*/s32[16]{0:T(128)S(1)}, s32[528]{0:T(1024)S(1)}, ...), branch_computations={%region_1.6_spmd, %region_6.7_spmd} | conditional | flops 12917111808 | bytes 165553760 | solution.py:622
  84.6 21.6 %purify_column.1 = f32[512,128]{1,0:T(8,128)S(1)} custom-call(s32[8]{0:T(128)S(1)} %get-tuple-element.74.blocks_ref, s32[264]{0:T(512)S(1)} %get-tuple-element.75.pn_ref, s32[264]{0:T(512)S(1)} %get-tuple-element.76.pt_ref, s32[528]{0:T(1024)S(1)} %get-tuple-element.77.an_ref, s32[528]{0:T(1024)S(1)} %get-tuple-element.78.at_ref, ...), custom_call_target="tpu_custom_call" | custom-call | tf_op jit(solution)/shard_map/cond/branch_1_fun/purify_column/pallas_call | solution.py:601
  106.2 0.0 copy-start.5
  106.2 0.7 copy-done.5
  (5 shorter events, 0.1 us)
Async XLA Ops:
  6.5 38.2 %copy-start.6 = (s32[32,32]{1,0:T(8,128)S(1)}, s32[32,32]{1,0:T(8,128)}, u32[]{:S(2)}) copy-start(s32[32,32]{1,0:T(8,128)} %pat_ref.3) | copy-start | bytes 12292
  9.2 10.9 %all-to-all-start.4 = ((f32[8,64,128]{2,1,0:T(8,128)}), f32[8,64,128]{2,1,0:T(8,128)S(1)}, u32[]{:S(2)}, u32[]{:S(2)}) async-start(f32[8,64,128]{2,1,0:T(8,128)} %bitcast.64), calls=%async_computation.8 | async-start | bytes 524288 | tf_op jit(solution)/shard_map/all_to_all | solution.py:596
  20.2 3.0 %collective-permute-start = (f32[32,128]{1,0:T(8,128)S(1)}, f32[32,128]{1,0:T(8,128)S(1)}, u32[]{:S(2)}, u32[]{:S(2)}) collective-permute-start(f32[32,128]{1,0:T(8,128)S(1)} %slice_select_fusion), channel_id=1, source_target_pairs={{0,2},{2,0},{4,6},{6,4},{8,10},{10,8},{12,14},{14,12},{16,18},{18,... | collective-permute-start | bytes 49160 | tf_op jit(solution)/shard_map/ppermute | solution.py:476
  42.4 9.5 %collective-permute-start.3 = (f32[512,128]{1,0:T(8,128)S(1)}, f32[512,128]{1,0:T(8,128)S(1)}, u32[]{:S(2)}, u32[]{:S(2)}) collective-permute-start(f32[512,128]{1,0:T(8,128)S(1)} %bitcast.60), channel_id=1, source_target_pairs={{0,1},{2,66},{4,5},{6,70},{8,9},{10,74},{12,13},{14,78},{16,17},{1... | collective-permute-start | bytes 786440 | tf_op jit(solution)/shard_map/ppermute | solution.py:476
  43.0 8.9 %collective-permute-start.2 = (f32[512,128]{1,0:T(8,128)S(1)}, f32[512,128]{1,0:T(8,128)S(1)}, u32[]{:S(2)}, u32[]{:S(2)}) collective-permute-start(f32[512,128]{1,0:T(8,128)S(1)} %bitcast.61), channel_id=1, source_target_pairs={{0,129},{2,98},{4,133},{6,102},{8,137},{10,106},{12,141},{14,110},... | collective-permute-start | bytes 786440 | tf_op jit(solution)/shard_map/ppermute | solution.py:476
  44.7 7.2 %collective-permute-start.1 = (f32[512,128]{1,0:T(8,128)S(1)}, f32[512,128]{1,0:T(8,128)S(1)}, u32[]{:S(2)}, u32[]{:S(2)}) collective-permute-start(f32[512,128]{1,0:T(8,128)S(1)} %bitcast.62), channel_id=1, source_target_pairs={{0,128},{2,34},{4,132},{6,38},{8,136},{10,42},{12,140},{14,46},{16... | collective-permute-start | bytes 786440 | tf_op jit(solution)/shard_map/ppermute | solution.py:476
  52.0 32.6 %copy-start.4 = (f32[512,128]{1,0:T(8,128)S(1)}, f32[512,128]{1,0:T(8,128)}, u32[]{:S(2)}) copy-start(f32[512,128]{1,0:T(8,128)} %tile_ref.1) | copy-start | bytes 786436
  52.0 17.7 %collective-permute-start.4 = (f32[1024,128]{1,0:T(8,128)S(1)}, f32[1024,128]{1,0:T(8,128)}, u32[]{:S(2)}, u32[]{:S(2)}) collective-permute-start(f32[1024,128]{1,0:T(8,128)S(1)} %get-tuple-element.195), channel_id=1, source_target_pairs={{0,32},{2,130},{4,36},{6,134},{8,40},{10,138},{12,44},{14,142},{16... | collective-permute-start | bytes 1572872 | tf_op jit(solution)/shard_map/ppermute | solution.py:476
  53.1 16.7 %collective-permute-start.5 = (f32[1024,128]{1,0:T(8,128)S(1)}, f32[1024,128]{1,0:T(8,128)}, u32[]{:S(2)}, u32[]{:S(2)}) collective-permute-start(f32[1024,128]{1,0:T(8,128)S(1)} %get-tuple-element.196), channel_id=1, source_target_pairs={{0,96},{2,131},{4,100},{6,135},{8,104},{10,139},{12,108},{14,143},... | collective-permute-start | bytes 1572872 | tf_op jit(solution)/shard_map/ppermute | solution.py:476
  53.7 26.9 %collective-permute-start.10 = (f32[2048,128]{1,0:T(8,128)S(1)}, f32[2048,128]{1,0:T(8,128)S(1)}, u32[]{:S(2)}, u32[]{:S(2)}) collective-permute-start(f32[2048,128]{1,0:T(8,128)S(1)} %pad_maximum_fusion), channel_id=1, source_target_pairs={{0,2},{2,0},{4,6},{6,4},{8,10},{10,8},{12,14},{14,12},{16,18},{18,... | collective-permute-start | bytes 3145736 | tf_op jit(solution)/shard_map/ppermute | solution.py:476
  58.3 13.5 %collective-permute-start.7 = (f32[1024,128]{1,0:T(8,128)S(1)}, f32[1024,128]{1,0:T(8,128)}, u32[]{:S(2)}, u32[]{:S(2)}) collective-permute-start(f32[1024,128]{1,0:T(8,128)S(1)} %get-tuple-element.195), channel_id=1, source_target_pairs={{0,96},{2,131},{4,100},{6,135},{8,104},{10,139},{12,108},{14,143},... | collective-permute-start | bytes 1572872 | tf_op jit(solution)/shard_map/ppermute | solution.py:476
  58.6 13.1 %collective-permute-start.6 = (f32[1024,128]{1,0:T(8,128)S(1)}, f32[1024,128]{1,0:T(8,128)}, u32[]{:S(2)}, u32[]{:S(2)}) collective-permute-start(f32[1024,128]{1,0:T(8,128)S(1)} %get-tuple-element.196), channel_id=1, source_target_pairs={{0,32},{2,130},{4,36},{6,134},{8,40},{10,138},{12,44},{14,142},{16... | collective-permute-start | bytes 1572872 | tf_op jit(solution)/shard_map/ppermute | solution.py:476
  69.8 8.4 %collective-permute-start.8 = (f32[1024,128]{1,0:T(8,128)}, f32[1024,128]{1,0:T(8,128)}, u32[]{:S(2)}, u32[]{:S(2)}) collective-permute-start(f32[1024,128]{1,0:T(8,128)} %collective-permute-done.4), channel_id=1, source_target_pairs={{0,32},{2,130},{4,36},{6,134},{8,40},{10,138},{12,44},{14,142},{16... | collective-permute-start | bytes 1572872 | tf_op jit(solution)/shard_map/ppermute | solution.py:476
  71.7 8.3 %collective-permute-start.9 = (f32[1024,128]{1,0:T(8,128)}, f32[1024,128]{1,0:T(8,128)}, u32[]{:S(2)}, u32[]{:S(2)}) collective-permute-start(f32[1024,128]{1,0:T(8,128)} %collective-permute-done.5), channel_id=1, source_target_pairs={{0,96},{2,131},{4,100},{6,135},{8,104},{10,139},{12,108},{14,143},... | collective-permute-start | bytes 1572872 | tf_op jit(solution)/shard_map/ppermute | solution.py:476
  71.7 8.9 %collective-permute-start.11 = (f32[1024,128]{1,0:T(8,128)}, f32[1024,128]{1,0:T(8,128)}, u32[]{:S(2)}, u32[]{:S(2)}) collective-permute-start(f32[1024,128]{1,0:T(8,128)} %collective-permute-done.4), channel_id=1, source_target_pairs={{0,2},{2,0},{4,6},{6,4},{8,10},{10,8},{12,14},{14,12},{16,18},{18,... | collective-permute-start | bytes 1572872 | tf_op jit(solution)/shard_map/ppermute | solution.py:476
  71.7 9.9 %collective-permute-start.12 = (f32[1024,128]{1,0:T(8,128)}, f32[1024,128]{1,0:T(8,128)}, u32[]{:S(2)}, u32[]{:S(2)}) collective-permute-start(f32[1024,128]{1,0:T(8,128)} %collective-permute-done.5), channel_id=1, source_target_pairs={{0,2},{2,0},{4,6},{6,4},{8,10},{10,8},{12,14},{14,12},{16,18},{18,... | collective-permute-start | bytes 1572872 | tf_op jit(solution)/shard_map/ppermute | solution.py:476
  80.1 2.3 %collective-permute-start.13 = (f32[1024,128]{1,0:T(8,128)}, f32[1024,128]{1,0:T(8,128)}, u32[]{:S(2)}, u32[]{:S(2)}) collective-permute-start(f32[1024,128]{1,0:T(8,128)} %collective-permute-done.6), channel_id=1, source_target_pairs={{0,2},{2,0},{4,6},{6,4},{8,10},{10,8},{12,14},{14,12},{16,18},{18,... | collective-permute-start | bytes 1572872 | tf_op jit(solution)/shard_map/ppermute | solution.py:476
  80.1 3.0 %collective-permute-start.14 = (f32[1024,128]{1,0:T(8,128)}, f32[1024,128]{1,0:T(8,128)}, u32[]{:S(2)}, u32[]{:S(2)}) collective-permute-start(f32[1024,128]{1,0:T(8,128)} %collective-permute-done.7), channel_id=1, source_target_pairs={{0,2},{2,0},{4,6},{6,4},{8,10},{10,8},{12,14},{14,12},{16,18},{18,... | collective-permute-start | bytes 1572872 | tf_op jit(solution)/shard_map/ppermute | solution.py:476
  80.6 3.2 %collective-permute-start.15 = (f32[1024,128]{1,0:T(8,128)}, f32[1024,128]{1,0:T(8,128)}, u32[]{:S(2)}, u32[]{:S(2)}) collective-permute-start(f32[1024,128]{1,0:T(8,128)} %collective-permute-done.8), channel_id=1, source_target_pairs={{0,2},{2,0},{4,6},{6,4},{8,10},{10,8},{12,14},{14,12},{16,18},{18,... | collective-permute-start | bytes 1572872 | tf_op jit(solution)/shard_map/ppermute | solution.py:476
  80.6 4.0 %collective-permute-start.16 = (f32[1024,128]{1,0:T(8,128)}, f32[1024,128]{1,0:T(8,128)}, u32[]{:S(2)}, u32[]{:S(2)}) collective-permute-start(f32[1024,128]{1,0:T(8,128)} %collective-permute-done.9), channel_id=1, source_target_pairs={{0,2},{2,0},{4,6},{6,4},{8,10},{10,8},{12,14},{14,12},{16,18},{18,... | collective-permute-start | bytes 1572872 | tf_op jit(solution)/shard_map/ppermute | solution.py:476
  106.2 0.7 copy-start.5
